TPU v7x, 32 devices: a whole 2x2x4 slice. The times are simulated.
32 devices in a mesh: ctx: 8 (over z, y), head: 4 (over x, core).
Axes of the slice: x: 2, y: 2, z: 4, core: 2. Of those that a mesh axis runs over, the one named last changes fastest.
Arguments:
- queries: bfloat16 [1024, 16384], P('ctx', 'head'), may hold values from -50 to 50
- keys: bfloat16 [1024, 1024], P('ctx', 'head'), may hold values from -4 to 4
- values: bfloat16 [1024, 1024], P('ctx', 'head'), may hold values from -6 to 6
- lengths: int32 [10], replicated, may hold values from 1 to 192, 1024 in all
- first_block: int32 [8], replicated, may hold values from 0 to 7, as said below
Outputs:
- attended: bfloat16 [1024, 16384], P(('ctx', 'head'))
Inputs may be any that keep to these rules, and one draw needn't show every extreme that they name: first_block[d] = (d + c) mod 8 for one c of the draw; index d of ctx holds the blocks first_block[d] and 15 - first_block[d] in that order.
All inputs are finite; a program needn't handle non-finite values.
Results may differ from a plain program's by a relative error of at most 0.004.
Values may be sent and summed in bfloat16 or wider, within the bound.
A program may use at most 64 MiB of HBM per device.

v0:
```python
import math

import jax
import jax.numpy as jnp
from jax import lax
from jax.sharding import PartitionSpec as P

DH = 128


lowest_score = -1e30


def shifted(value, axis, steps):
    count = lax.axis_size(axis)
    pairs = [(source, (source + steps) % count) for source in range(count)]
    return lax.ppermute(value, axis, pairs)


def reach_levels(devices):
    levels = 0
    for power in range(2, 6):
        levels += min(1, devices // 2**power)
    return levels


def key_width(length):
    for width in range(min(length, 512), 0, -1):
        if length % width == 0 and width % 128 == 0:
            return width
    for width in range(min(length, 512), 0, -1):
        if length % width == 0:
            return width
    return length


def locate(rows, first_block, lengths, block, pairs):
    device = rows // (2 * block)
    offset = rows % (2 * block)
    table = device[:, None] == jnp.arange(pairs, dtype=jnp.int32)[None, :]
    leading = jnp.sum(jnp.where(table, first_block[None, :], 0), axis=1)
    which = jnp.where(offset < block, leading, 2 * pairs - 1 - leading)
    position = which * block + offset % block
    ends = jnp.cumsum(lengths)
    document = jnp.sum((ends[None, :] <= position[:, None]).astype(jnp.int32), axis=1)
    return (position, document)


def attend(state, pieces, allowed, grouped, kv_local):

    def work(carry):
        maxima, totals, accum = carry
        count = pieces.shape[0]
        key_part = pieces[:, : kv_local * DH].reshape(count, kv_local, DH)
        value_part = pieces[:, kv_local * DH :].reshape(count, kv_local, DH)
        scores = jnp.einsum(
            "qhgd,khd->qhgk", grouped, key_part, preferred_element_type=jnp.float32
        ) * (1.0 / math.sqrt(DH))
        gate = allowed[:, None, None, :]
        masked = jnp.where(gate, scores, lowest_score)
        highest = jnp.maximum(maxima, jnp.max(masked, axis=-1))
        expo = jnp.where(gate, jnp.exp(masked - highest[..., None]), 0.0)
        factor = jnp.exp(maxima - highest)
        totals = totals * factor + jnp.sum(expo, axis=-1)
        accum = accum * factor[..., None] + jnp.einsum(
            "qhgk,khd->qhgd",
            expo.astype(jnp.bfloat16),
            value_part,
            preferred_element_type=jnp.float32,
        )
        return (highest, totals, accum)

    def unchanged(carry):
        return carry

    return lax.cond(jnp.any(allowed), work, unchanged, state)


def shards(queries, keys, values, lengths, first_block):
    rows_here = queries.shape[0]
    block = rows_here // 2
    kv_local = keys.shape[1] // DH
    per_group = queries.shape[1] // (kv_local * DH)
    pairs = lax.axis_size("ctx")
    device = lax.axis_index("ctx")
    own_rows = device * rows_here + jnp.arange(rows_here, dtype=jnp.int32)
    query_pos, query_doc = locate(own_rows, first_block, lengths, block, pairs)
    grouped = queries.reshape(rows_here, kv_local, per_group, DH)
    stacked = jnp.concatenate([keys, values], axis=1)
    start_state = (
        jnp.full((rows_here, kv_local, per_group), lowest_score, jnp.float32),
        jnp.zeros((rows_here, kv_local, per_group), jnp.float32),
        jnp.zeros((rows_here, kv_local, per_group, DH), jnp.float32),
    )

    def sweep(state, pieces, rows):
        width = key_width(pieces.shape[0])

        def turn(level, carry):
            begin = level * width
            part = lax.dynamic_slice_in_dim(pieces, begin, width, 0)
            part_rows = lax.dynamic_slice_in_dim(rows, begin, width, 0)
            key_pos, key_doc = locate(part_rows, first_block, lengths, block, pairs)
            allowed = (key_doc[None, :] == query_doc[:, None]) & (
                key_pos[None, :] <= query_pos[:, None]
            )
            return attend(carry, part, allowed, grouped, kv_local)

        return lax.fori_loop(0, pieces.shape[0] // width, turn, state)

    levels = reach_levels(pairs)
    lower = stacked[:block]
    upper = stacked
    for level in range(levels):
        lower = jnp.concatenate([shifted(lower, "ctx", 1 << level), lower], axis=0)
        upper = jnp.concatenate([upper, shifted(upper, "ctx", -(1 << level))], axis=0)
    span = (1 << levels) - 1
    above = (device + jnp.arange(0, span + 1, dtype=jnp.int32)) % pairs
    upper_rows = (
        above[:, None] * rows_here + jnp.arange(rows_here, dtype=jnp.int32)[None, :]
    ).reshape(-1)
    below = (device + jnp.arange(-span, 0, dtype=jnp.int32)) % pairs
    lower_rows = (below[:, None] * rows_here + jnp.arange(block, dtype=jnp.int32)[None, :]).reshape(
        -1
    )
    state = sweep(start_state, upper, upper_rows)
    state = sweep(state, lower[: span * block], lower_rows)
    maxima, totals, accum = state
    attended = (
        (accum / totals[..., None])
        .reshape(rows_here, kv_local * per_group * DH)
        .astype(jnp.bfloat16)
    )
    return lax.all_to_all(attended, "head", split_axis=0, concat_axis=1, tiled=True)


def solution(mesh):
    in_specs = (P("ctx", "head"), P("ctx", "head"), P("ctx", "head"), P(), P())
    out_specs = P(("ctx", "head"), None)
    return jax.shard_map(shards, mesh=mesh, in_specs=in_specs, out_specs=out_specs, check_vma=False)
```

profile of v0, /device:TPU:0, one launch (start us, length us, event | category | flops | bytes accessed | tf_op | source)
XLA Modules:
  0.0 63.4 jit_solution(8147171807847945698)
XLA Ops:
  0.0 0.8 %constant_dynamic-update-slice_fusion.1 = bf16[128,512]{1,0:T(8,128)(2,1)S(1)} fusion(bf16[128,256]{1,0:T(8,128)(2,1)} %param.10), kind=kLoop, calls=%fused_computation.47 | loop fusion | bytes 131072
  0.8 0.8 %constant_dynamic-update-slice_fusion = bf16[128,512]{1,0:T(8,128)(2,1)S(1)} fusion(bf16[128,512]{1,0:T(8,128)(2,1)S(1)} %constant_dynamic-update-slice_fusion.1, bf16[128,256]{1,0:T(8,128)(2,1)} %param.11), kind=kLoop, calls=%fused_computation.46 | loop fusion | bytes 131072 | tf_op jit(solution)/shard_map/concatenate | solution.py:89
  1.7 6.0 %collective-permute-start = (bf16[128,512]{1,0:T(8,128)(2,1)S(1)}, bf16[128,512]{1,0:T(8,128)(2,1)S(1)}, u32[]{:S(2)}, u32[]{:S(2)}) collective-permute-start(bf16[128,512]{1,0:T(8,128)(2,1)S(1)} %constant_dynamic-update-slice_fusion), channel_id=1, source_target_pairs={{0,28},{4,0},{8,4},{12,8},{16,12},{20,16},{24,20},{28,24},{1,29},{... | collective-permute-start | bytes 393224 | tf_op jit(solution)/shard_map/ppermute | solution.py:17
  7.8 0.7 %select_reduce_fusion.2 = s32[128]{0:T(128)S(1)} fusion(s32[8]{0:T(128)} %param.13, s32[128]{0:T(128)S(1)} %and_select_fusion.2), kind=kLoop, calls=%fused_computation.48 | loop fusion | flops 2944 | bytes 1056 | tf_op jit(solution)/shard_map/reduce_sum | solution.py:41
  8.6 0.7 %select_reduce_fusion = s32[512]{0:T(512)S(1)} fusion(s32[8]{0:T(128)} %param.13, s32[512]{0:T(512)S(1)} %add_select_fusion.1), kind=kLoop, calls=%fused_computation.40 | loop fusion | flops 11776 | bytes 4128 | tf_op jit(solution)/shard_map/while/body/eval_jaxpr/reduce_sum | solution.py:41
  9.3 0.1 fusion.27
  9.4 0.8 %reduce-window.8 = s32[10,1]{0,1:T(1,128)S(1)} reduce-window(s32[10,1]{0,1:T(1,128)} %bitcast.88, s32[]{:T(128)} %constant.175.clone.1), window={size=10x1 pad=9_0x0_0}, to_apply=%region_0.1 | reduce-window | flops 90 | bytes 84 | tf_op jit(solution)/shard_map/reduce-window.3
  10.3 0.1 convert_reduce_fusion.2
  10.6 0.7 %select_reduce_fusion.1 = s32[192]{0:T(256)S(1)} fusion(s32[8]{0:T(128)} %param.13, s32[192]{0:T(256)S(1)} %and_select_fusion.5), kind=kLoop, calls=%fused_computation.44 | loop fusion | flops 4416 | bytes 1568 | tf_op jit(solution)/shard_map/while/body/eval_jaxpr/reduce_sum | solution.py:41
  11.4 0.8 %fusion.41 = (pred[]{:T(512)}, pred[128,512]{0,1:T(8,128)(4,1)S(1)}) fusion(s32[128]{0:T(128)S(1)} %fusion.35, s32[512]{0:T(512)S(1)} %fusion.27, s32[128]{0:T(128)S(1)} %convert_reduce_fusion.2, s32[512]{0:T(512)S(1)} %convert_reduce_fusion), kind=kLoop, calls=%fused_computation.105 | loop fusion | flops 262143 | bytes 70657 | tf_op jit(solution)/shard_map/while/body/eval_jaxpr/reduce_or | solution.py:76
  12.3 1.6 %copy.33 = bf16[128,4096]{0,1:T(8,128)(2,1)S(1)} copy(bf16[128,4096]{1,0:T(8,128)(2,1)} %param.9) | data formatting | bytes 2097152 | tf_op args[0]
  14.6 0.1 collective-permute-done.2
  14.8 3.9 %collective-permute-start.1 = (bf16[256,512]{1,0:T(8,128)(2,1)S(1)}, bf16[256,512]{1,0:T(8,128)(2,1)S(1)}, u32[]{:S(2)}, u32[]{:S(2)}) collective-permute-start(bf16[256,512]{1,0:T(8,128)(2,1)S(1)} %pad_maximum_fusion.1), channel_id=1, source_target_pairs={{0,24},{4,28},{8,0},{12,4},{16,8},{20,12},{24,16},{28,20},{1,25},{... | collective-permute-start | bytes 786440 | tf_op jit(solution)/shard_map/ppermute | solution.py:17
  18.6 0.7 %fusion.42 = (pred[]{:T(512)}, pred[128,192]{0,1:T(8,128)(4,1)S(1)}) fusion(s32[128]{0:T(128)S(1)} %fusion.35, s32[192]{0:T(256)S(1)} %fusion.32, s32[128]{0:T(128)S(1)} %convert_reduce_fusion.2, s32[192]{0:T(256)S(1)} %convert_reduce_fusion.1), kind=kLoop, calls=%fused_computation.106 | loop fusion | flops 98303 | bytes 27137 | tf_op jit(solution)/shard_map/while/body/eval_jaxpr/reduce_or | solution.py:76
  20.0 1.6 %broadcast_in_dim.152 = f32[128,2,16,128]{3,0,2,1:T(8,128)} broadcast(f32[]{:T(128)} %constant.190.clone.1), dimensions={} | broadcast | bytes 2097156 | tf_op jit(solution)/shard_map/broadcast_in_dim | solution.py:93
  21.6 1.3 %collective-permute-done.3 = bf16[128,512]{1,0:T(8,128)(2,1)S(1)} collective-permute-done((bf16[128,512]{1,0:T(8,128)(2,1)S(1)}, bf16[128,512]{1,0:T(8,128)(2,1)S(1)}, u32[]{:S(2)}, u32[]{:S(2)}) %collective-permute-start.3) | collective-permute-done | bytes 131104 | tf_op jit(solution)/shard_map/ppermute | solution.py:17
  23.0 2.3 %collective-permute-done.1 = bf16[256,512]{1,0:T(8,128)(2,1)S(1)} collective-permute-done((bf16[256,512]{1,0:T(8,128)(2,1)S(1)}, bf16[256,512]{1,0:T(8,128)(2,1)S(1)}, u32[]{:S(2)}, u32[]{:S(2)}) %collective-permute-start.1) | collective-permute-done | bytes 262176 | tf_op jit(solution)/shard_map/ppermute | solution.py:17
  25.4 9.3 %conditional.2 = ((f32[128,2,16]{0,2,1:T(8,128)S(1)}, f32[128,2,16]{0,2,1:T(8,128)S(1)}, f32[128,2,16,128]{3,0,2,1:T(8,128)})) conditional(s32[]{:T(128)} %convert_element_type.37, (f32[128,2,16]{0,2,1:T(8,128)S(1)}, f32[128,2,16]{0,2,1:T(8,128)S(1)}, f32[128,2,16,128]{3,0,2,1:T(8,128)}) %tuple.28, (pred[128,512]{0,1:T(8,128)(4,1)S(1)}, ...), branch_computations={%region_9.10_spmd, %region_10.13_spmd} | conditional | flops 1102061568 | bytes 33488928 | solution.py:76
  25.4 0.2 copy.34
  25.6 1.4 %fusion = (f32[128,2,16]{0,2,1:T(8,128)S(1)}, f32[2,512,128,16]{2,1,3,0:T(8,128)S(1)}) fusion(pred[128,512]{0,1:T(8,128)(4,1)S(1)} %get-tuple-element.113, bf16[512,2,128,1]{0,2,3,1:T(8,128)(2,1)S(1)} %bitcast.81, bf16[128,2,16,128]{0,3,2,1:T(8,128)(2,1)S(1)} %get-tuple-element.174), kind=kOutput, calls=%fused_computation.2 | convolution fusion | flops 543158272 | bytes 9781248 | tf_op jit(solution)/shard_map/while/body/eval_jaxpr/cond/branch_1_fun/qhgd,khd->qhgk/dot_general | solution.py:56
  27.0 2.1 %fusion.2 = f32[128,2,16]{0,2,1:T(8,128)S(1)} fusion(f32[2,512,128,16]{2,1,3,0:T(8,128)S(1)} %get-tuple-element.195, f32[128,2,16]{0,2,1:T(8,128)S(1)} %max.5, pred[128,512]{0,1:T(8,128)(4,1)S(1)} %get-tuple-element.113), kind=kLoop, calls=%fused_computation.4 | loop fusion | flops 10481664 | bytes 8486912 | tf_op jit(solution)/shard_map/while/body/eval_jaxpr/cond/branch_1_fun/reduce_sum | solution.py:64
  29.2 5.5 %bitcast_add_fusion = f32[128,2,16,128]{3,0,2,1:T(8,128)} fusion(f32[128,2,16,128]{3,0,2,1:T(8,128)} %get-tuple-element.117, bf16[512,2,128,1]{0,2,3,1:T(8,128)(2,1)S(1)} %bitcast.84, f32[2,512,128,16]{2,1,3,0:T(8,128)S(1)} %get-tuple-element.195, f32[128,2,16]{0,2,1:T(8,128)S(1)} %max.5, pred[128,512]{0,1:T(8,128)(4,1)S(1)} %get-tuple-element.113, ...), kind=kOutput, calls=%fused_computation.7 | convolution fusion | flops 548405248 | bytes 12943360 | tf_op jit(solution)/shard_map/while/body/eval_jaxpr/cond/branch_1_fun/qhgk,khd->qhgd/dot_general | solution.py:65
  34.7 7.5 %conditional.3 = ((f32[128,2,16]{0,2,1:T(8,128)S(1)}, f32[128,2,16,128]{3,0,2,1:T(8,128)})) conditional(s32[]{:T(128)} %convert_element_type.35, (f32[128,2,16]{0,2,1:T(8,128)S(1)}, f32[128,2,16,128]{3,0,2,1:T(8,128)}) %tuple.30, (pred[128,192]{0,1:T(8,128)(4,1)S(1)}, bf16[192,512]{1,0:T(8,128)(2,1)S(1)}, bf16[128,2,16,128]{0,3,2,1:T(8,128)(2,1)S(1)}, ...), branch_computations={%region_13.14_spmd, %region_14.17_spmd} | conditional | flops 413933568 | bytes 20160564 | solution.py:76
  34.7 0.9 %copy-done = bf16[128,2,16,128]{0,3,2,1:T(8,128)(2,1)} copy-done((bf16[128,2,16,128]{0,3,2,1:T(8,128)(2,1)}, bf16[128,2,16,128]{0,3,2,1:T(8,128)(2,1)S(1)}, u32[]{:S(2)}) %copy-start) | copy-done | bytes 1048600 | tf_op jit(solution)/shard_map/while/body/eval_jaxpr/cond
  35.7 1.8 %fusion.11 = (f32[128,2,16]{0,2,1:T(8,128)S(1)}, f32[2,192,128,16]{2,1,3,0:T(8,128)S(1)}) fusion(pred[128,192]{0,1:T(8,128)(4,1)S(1)} %get-tuple-element.132, bf16[128,2,16,128]{0,3,2,1:T(8,128)(2,1)} %copy-done, bf16[192,2,128,1]{2,1,0,3:T(2,128)(2,1)S(1)} %bitcast.83), kind=kOutput, calls=%fused_computation.15 | convolution fusion | flops 203681792 | bytes 4333568 | tf_op jit(solution)/shard_map/while/body/eval_jaxpr/cond/branch_1_fun/qhgd,khd->qhgk/dot_general | solution.py:56
  37.5 0.8 %fusion.13 = f32[128,2,16]{0,2,1:T(8,128)S(1)} fusion(f32[2,192,128,16]{2,1,3,0:T(8,128)S(1)} %get-tuple-element.199, f32[128,2,16]{0,2,1:T(8,128)S(1)} %max.6, pred[128,192]{0,1:T(8,128)(4,1)S(1)} %get-tuple-element.132), kind=kLoop, calls=%fused_computation.17 | loop fusion | flops 3928064 | bytes 3203072 | tf_op jit(solution)/shard_map/while/body/eval_jaxpr/cond/branch_1_fun/reduce_sum | solution.py:64
  38.4 3.9 %bitcast_add_fusion.1 = f32[128,2,16,128]{3,0,2,1:T(8,128)} fusion(f32[128,2,16,128]{3,0,2,1:T(8,128)} %get-tuple-element.137, f32[2,192,128,16]{2,1,3,0:T(8,128)S(1)} %get-tuple-element.199, f32[128,2,16]{0,2,1:T(8,128)S(1)} %max.6, pred[128,192]{0,1:T(8,128)(4,1)S(1)} %get-tuple-element.132, f32[128,2,16]{0,2,1:T(8,128)S(1)} %get-tuple-element.187, ...), kind=kOutput, calls=%fused_computation.18 | convolution fusion | flops 206307328 | bytes 7495680 | tf_op jit(solution)/shard_map/while/body/eval_jaxpr/cond/branch_1_fun/qhgk,khd->qhgd/dot_general | solution.py:65
  42.2 1.9 %divide_convert_fusion = bf16[128,2,16,128]{3,0,2,1:T(8,128)(2,1)S(1)} fusion(f32[128,2,16,128]{3,0,2,1:T(8,128)} %get-tuple-element.146, f32[128,2,16]{0,2,1:T(8,128)S(1)} %get-tuple-element.147), kind=kLoop, calls=%fused_computation.32 | loop fusion | flops 1048576 | bytes 3162112 | tf_op jit(solution)/shard_map/convert_element_type | solution.py:132
  44.2 0.7 %copy.37 = bf16[128,2,16,128]{3,2,1,0:T(8,128)(2,1)S(1)} copy(bf16[128,2,16,128]{3,0,2,1:T(8,128)(2,1)S(1)} %divide_convert_fusion) | data formatting | bytes 2097152 | tf_op jit(solution)/shard_map/convert_element_type | solution.py:132
  44.9 0.5 convert_element_type.39
  45.4 17.0 %all_to_all.16 = bf16[4,32,4096]{2,1,0:T(8,128)(2,1)S(1)} all-to-all(bf16[4,32,4096]{2,1,0:T(8,128)(2,1)S(1)} %convert_element_type.39), channel_id=1, replica_groups=mesh['ctx'=8,'head'=4] {'head'}, dimensions={0} | all-to-all | bytes 2097152 | tf_op jit(solution)/shard_map/all_to_all | solution.py:134
  62.4 1.0 %copy.54 = bf16[4,4,8,4096]{3,2,0,1:T(8,128)(2,1)} copy(bf16[4,4,8,4096]{3,2,1,0:T(8,128)(2,1)S(1)} %bitcast.80) | data formatting | bytes 2097152 | tf_op jit(solution)/shard_map/all_to_all | solution.py:134
  (31 shorter events, 0.8 us)
Async XLA Ops:
  1.7 13.1 %collective-permute-start = (bf16[128,512]{1,0:T(8,128)(2,1)S(1)}, bf16[128,512]{1,0:T(8,128)(2,1)S(1)}, u32[]{:S(2)}, u32[]{:S(2)}) collective-permute-start(bf16[128,512]{1,0:T(8,128)(2,1)S(1)} %constant_dynamic-update-slice_fusion), channel_id=1, source_target_pairs={{0,28},{4,0},{8,4},{12,8},{16,12},{20,16},{24,20},{28,24},{1,29},{... | collective-permute-start | bytes 393224 | tf_op jit(solution)/shard_map/ppermute | solution.py:17
  7.7 7.0 %collective-permute-start.2 = (bf16[64,512]{1,0:T(8,128)(2,1)S(1)}, bf16[64,512]{1,0:T(8,128)(2,1)S(1)}, u32[]{:S(2)}, u32[]{:S(2)}) collective-permute-start(bf16[64,512]{1,0:T(8,128)(2,1)S(1)} %slice.22), channel_id=1, source_target_pairs={{0,4},{4,8},{8,12},{12,16},{16,20},{20,24},{24,28},{28,0},{1,5},{5... | collective-permute-start | bytes 196616 | tf_op jit(solution)/shard_map/ppermute | solution.py:17
  14.7 8.3 %collective-permute-start.3 = (bf16[128,512]{1,0:T(8,128)(2,1)S(1)}, bf16[128,512]{1,0:T(8,128)(2,1)S(1)}, u32[]{:S(2)}, u32[]{:S(2)}) collective-permute-start(bf16[128,512]{1,0:T(8,128)(2,1)S(1)} %pad_maximum_fusion.3), channel_id=1, source_target_pairs={{0,8},{4,12},{8,16},{12,20},{16,24},{20,28},{24,0},{28,4},{1,9},{5... | collective-permute-start | bytes 393224 | tf_op jit(solution)/shard_map/ppermute | solution.py:17
  14.8 10.5 %collective-permute-start.1 = (bf16[256,512]{1,0:T(8,128)(2,1)S(1)}, bf16[256,512]{1,0:T(8,128)(2,1)S(1)}, u32[]{:S(2)}, u32[]{:S(2)}) collective-permute-start(bf16[256,512]{1,0:T(8,128)(2,1)S(1)} %pad_maximum_fusion.1), channel_id=1, source_target_pairs={{0,24},{4,28},{8,0},{12,4},{16,8},{20,12},{24,16},{28,20},{1,25},{... | collective-permute-start | bytes 786440 | tf_op jit(solution)/shard_map/ppermute | solution.py:17
  34.7 1.0 %copy-start = (bf16[128,2,16,128]{0,3,2,1:T(8,128)(2,1)}, bf16[128,2,16,128]{0,3,2,1:T(8,128)(2,1)S(1)}, u32[]{:S(2)}) copy-start(bf16[128,2,16,128]{0,3,2,1:T(8,128)(2,1)S(1)} %get-tuple-element.180) | copy-start | bytes 3145732 | tf_op jit(solution)/shard_map/while/body/eval_jaxpr/cond
where the time goes:
time: 63.9 us; the launch traced here: 63.4 us
  blocking collectives  17 us (27%)
  matrix products  12.5 us (20%)
  other arithmetic  10.2 us (16%)
  starting transfers between devices  9.92 us (16%)
  local copies, waits for them, and re-layouts  8.45 us (13%)
  waiting for transfers between devices  3.77 us (6%)
  between operations  1.4 us (2%)
    all_to_all x1, blocking collectives, shards(): lax.all_to_all(attended, 'head', split_axis=0, concat_axis=1, tiled=True)  17 us
    ppermute x4, starting transfers between devices, shifted(): return lax.ppermute(value, axis, pairs)  9.92 us
    dot_general x2, matrix products, work(): jnp.einsum('qhgk,khd->qhgd', expo.astype(jnp.bfloat16), value_part, prefe...  9.34 us
    ppermute x4, waiting for transfers between devices, shifted(): return lax.ppermute(value, axis, pairs)  3.77 us
    dot_general x2, matrix products, work(): jnp.einsum('qhgd,khd->qhgk', grouped, key_part, preferred_element_type=jn...  3.19 us
    reduce_sum x2, other arithmetic, work(): totals = totals * factor + jnp.sum(expo, axis=-1)  2.95 us
    unnamed x2, local copies, waits for them, and re-layouts  2.46 us
    reduce_sum x3, other arithmetic, locate(): leading = jnp.sum(jnp.where(table, first_block[None, :], 0), axis=1)  2.22 us
  transfers between devices with their start and end apart: 4, of which 3 were waited for; matrix products, arithmetic and copies ran while one was open for 14% of the time, Pallas kernels for 0%

commit v1 on v0

v1 whole, which is shorter than its diff:
```python
import functools
import math

import jax
import jax.numpy as jnp
from jax import lax
from jax.experimental import pallas as pl
from jax.experimental.pallas import tpu as pltpu
from jax.sharding import PartitionSpec as P

DH = 128
LOWEST = -1e30
MESH = pl.DeviceIdType.MESH


def reach(devices):
    levels = 0
    for power in range(2, 6):
        levels += min(1, devices // 2**power)
    return (1 << levels) - 1


def kernel(
    pairs, heads, span, kv_local, per_group, chunk, tile,
    lengths_ref, first_ref, q_hbm, k_ref, v_ref, out_ref,
    q_buf, own, upper, windows, bias, obuf,
    q_sem, up_send, up_recv, down_send, down_recv, out_send, out_recv, self_sem,
):
    device = lax.axis_index("ctx")
    group = lax.axis_index("head")
    rows_here = q_buf.shape[0]
    block = rows_here // 2
    share = rows_here // heads
    dests = block // share
    chunks = per_group // chunk
    width = chunk * DH
    keys_seen = (span + 1) * block

    load_q = pltpu.make_async_copy(q_hbm, q_buf, q_sem)
    load_q.start()

    def around(step):
        return lax.rem(device + (step + pairs), pairs)

    def slot(back):
        return pl.ds((span - back) * block, block)

    barrier = pltpu.get_barrier_semaphore()
    for step in range(1, span + 1):
        pl.semaphore_signal(barrier, inc=1, device_id={"ctx": around(step)}, device_id_type=MESH)
        pl.semaphore_signal(barrier, inc=1, device_id={"ctx": around(-step)}, device_id_type=MESH)
    for step in range(1, heads):
        pl.semaphore_signal(
            barrier, inc=1, device_id={"head": lax.rem(group + step, heads)}, device_id_type=MESH
        )
    for h in range(kv_local):
        own[h, :, :DH] = k_ref[:, h * DH : (h + 1) * DH]
        own[h, :, DH:] = v_ref[:, h * DH : (h + 1) * DH]
    pl.semaphore_wait(barrier, 2 * span + heads - 1)

    def up_copy(h, step):
        return pltpu.make_async_remote_copy(
            src_ref=own.at[h, pl.ds(0, block)],
            dst_ref=windows.at[h, 0, slot(step)],
            send_sem=up_send.at[h, step - 1],
            recv_sem=up_recv.at[h, step - 1],
            device_id={"ctx": around(step)},
            device_id_type=MESH,
        )

    def down_copy(h, step):
        part = pl.ds(0, rows_here) if step < span else pl.ds(block, block)
        return pltpu.make_async_remote_copy(
            src_ref=own.at[h, part],
            dst_ref=upper.at[h, step - 1, part],
            send_sem=down_send.at[h, step - 1],
            recv_sem=down_recv.at[h, step - 1],
            device_id={"ctx": around(-step)},
            device_id_type=MESH,
        )

    for h in range(kv_local):
        for step in range(span, 0, -1):
            up_copy(h, step).start()
            down_copy(h, step).start()

    first = first_ref[device]
    shape = (block, keys_seen)
    offset = lax.broadcasted_iota(jnp.int32, shape, 0)
    place = lax.broadcasted_iota(jnp.int32, shape, 1)
    for which in range(2):
        at = first if which == 0 else 2 * pairs - 1 - first
        query_pos = at * block + offset
        key_pos = (at - span) * block + place
        begin = jnp.zeros(shape, jnp.int32)
        end = jnp.int32(0)
        for j in range(lengths_ref.shape[0]):
            end = end + lengths_ref[j]
            ends = jnp.full(shape, end, jnp.int32)
            begin = jnp.where(ends <= query_pos, ends, begin)
        allowed = (key_pos >= begin) & (key_pos <= query_pos)
        bias[which] = jnp.where(allowed, 0.0, LOWEST)
    for h in range(kv_local):
        windows[h, 0, slot(0)] = own[h, :block]
        windows[h, 1, slot(0)] = own[h, block:]

    def arrived(h):
        for step in range(1, span + 1):
            up_copy(h, step).wait_recv()
            down_copy(h, step).wait_recv()
        mine = jnp.full((block, 2 * DH), first, jnp.int32)
        for back in range(1, span + 1):
            piece = upper[h, back - 1, block:].astype(jnp.float32)
            for away in range(1 - back, back, 2):
                if away > 0:
                    other = upper[h, away - 1, :block]
                elif away == 0:
                    other = own[h, :block]
                else:
                    other = windows[h, 0, slot(-away)]
                holder = (2 * pairs - 1 - back - away) // 2
                piece = jnp.where(mine == holder, other.astype(jnp.float32), piece)
            windows[h, 1, slot(back)] = piece.astype(jnp.bfloat16)

    factor = math.log2(math.e) / math.sqrt(DH)

    def out_copy(step, dest, row, column, index):
        source = lax.rem(group, heads) * (kv_local * per_group * DH) + column
        return pltpu.make_async_remote_copy(
            src_ref=obuf.at[pl.ds(row, share), pl.ds(column, width)],
            dst_ref=out_ref.at[:, pl.ds(pl.multiple_of(source, DH), width)],
            send_sem=out_send.at[step, index],
            recv_sem=out_recv.at[step, index],
            device_id={"head": dest},
            device_id_type=MESH,
        )

    def self_copy(column, index):
        row = pl.multiple_of(group * share, share)
        target = group * (kv_local * per_group * DH) + column
        return pltpu.make_async_copy(
            obuf.at[pl.ds(row, share), pl.ds(column, width)],
            out_ref.at[:, pl.ds(pl.multiple_of(target, DH), width)],
            self_sem.at[index],
        )

    def attend(which, h, c):
        row = pl.multiple_of(which * block, block)
        column = pl.multiple_of((h * chunks + c) * width, width)
        key = windows[h, which, :, :DH]
        value = windows[h, which, :, DH:]
        gate = jnp.concatenate([bias[which]] * tile, axis=0)
        for part in range(chunk // tile):
            at = [column + (part * tile + i) * DH for i in range(tile)]
            query = jnp.concatenate(
                [q_buf[pl.ds(row, block), pl.ds(pl.multiple_of(a, DH), DH)] for a in at], axis=0
            )
            scores = gate + lax.dot_general(
                query, key, (((1,), (1,)), ((), ())), preferred_element_type=jnp.float32
            )
            highest = jnp.max(scores, axis=1, keepdims=True)
            expo = jnp.exp2((scores - highest) * factor)
            total = jnp.sum(expo, axis=1, keepdims=True)
            mixed = jnp.dot(
                expo.astype(jnp.bfloat16), value, preferred_element_type=jnp.float32
            )
            mixed = (mixed / total).astype(jnp.bfloat16)
            for i, a in enumerate(at):
                obuf[pl.ds(row, block), pl.ds(pl.multiple_of(a, DH), DH)] = mixed[
                    i * block : (i + 1) * block
                ]
        index = h * chunks + c
        for t in range(dests):
            dest = which * dests + t
            step = lax.rem(dest - group + heads, heads)

            @pl.when(step != 0)
            def _():
                spot = pl.multiple_of(dest * share, share)
                out_copy(step, dest, spot, column, index).start()

            @pl.when(step == 0)
            def _():
                self_copy(column, index).start()

    here = (group * share) // block
    load_q.wait()
    for turn in range(2):
        which = 1 - here if turn == 0 else here
        for h in range(kv_local):
            if turn == 0:
                arrived(h)

            @pl.loop(0, chunks)
            def _(c):
                attend(which, h, c)

    for h in range(kv_local):
        for step in range(1, span + 1):
            up_copy(h, step).wait_send()
            down_copy(h, step).wait_send()
    for index in range(kv_local * chunks):
        column = index * width
        self_copy(column, index).wait()
        for step in range(1, heads):
            dest = lax.rem(group + step, heads)
            spot = pl.multiple_of(dest * share, share)
            out_copy(step, dest, spot, column, index).wait_send()
            sender = lax.rem(group - step + heads, heads)
            target = sender * (kv_local * per_group * DH) + column
            pltpu.make_async_remote_copy(
                src_ref=obuf.at[pl.ds(spot, share), pl.ds(column, width)],
                dst_ref=out_ref.at[:, pl.ds(pl.multiple_of(target, DH), width)],
                send_sem=out_send.at[step, index],
                recv_sem=out_recv.at[step, index],
                device_id={"head": dest},
                device_id_type=MESH,
            ).wait_recv()


def shards(queries, keys, values, lengths, first_block):
    rows_here = queries.shape[0]
    block = rows_here // 2
    kv_local = keys.shape[1] // DH
    per_group = queries.shape[1] // (kv_local * DH)
    pairs = lax.axis_size("ctx")
    heads = lax.axis_size("head")
    span = reach(pairs)
    keys_seen = (span + 1) * block
    chunk = max(per_group // 2, 1)
    tile = max(1, min(chunk, 1024 // keys_seen))
    count = kv_local * (per_group // chunk)
    body = functools.partial(
        kernel, pairs, heads, span, kv_local, per_group, chunk, tile
    )
    vmem = pl.BlockSpec(memory_space=pltpu.VMEM)
    smem = pl.BlockSpec(memory_space=pltpu.SMEM)
    hbm = pl.BlockSpec(memory_space=pl.ANY)
    return pl.pallas_call(
        body,
        out_shape=jax.ShapeDtypeStruct(
            (rows_here // heads, queries.shape[1] * heads), jnp.bfloat16
        ),
        in_specs=[smem, smem, hbm, vmem, vmem],
        out_specs=hbm,
        scratch_shapes=[
            pltpu.VMEM(queries.shape, jnp.bfloat16),
            pltpu.VMEM((kv_local, rows_here, 2 * DH), jnp.bfloat16),
            pltpu.VMEM((kv_local, span, rows_here, 2 * DH), jnp.bfloat16),
            pltpu.VMEM((kv_local, 2, keys_seen, 2 * DH), jnp.bfloat16),
            pltpu.VMEM((2, block, keys_seen), jnp.float32),
            pltpu.VMEM(queries.shape, jnp.bfloat16),
            pltpu.SemaphoreType.DMA,
            pltpu.SemaphoreType.DMA((kv_local, span)),
            pltpu.SemaphoreType.DMA((kv_local, span)),
            pltpu.SemaphoreType.DMA((kv_local, span)),
            pltpu.SemaphoreType.DMA((kv_local, span)),
            pltpu.SemaphoreType.DMA((heads, count)),
            pltpu.SemaphoreType.DMA((heads, count)),
            pltpu.SemaphoreType.DMA((count,)),
        ],
        compiler_params=pltpu.CompilerParams(
            collective_id=0, has_side_effects=True, vmem_limit_bytes=32 * 2**20
        ),
    )(lengths, first_block, queries, keys, values)


def solution(mesh):
    in_specs = (P("ctx", "head"), P("ctx", "head"), P("ctx", "head"), P(), P())
    out_specs = P(("ctx", "head"), None)
    return jax.shard_map(shards, mesh=mesh, in_specs=in_specs, out_specs=out_specs, check_vma=False)
```

time: 63.9 us -> 32.6 us (0.51)
  the two profiles are of different devices: /device:TPU:0 before, /device:TPU:13 now
where the time goes in v1:
time: 32.6 us; the launch traced here: 32.3 us
  Pallas kernels  27.1 us (83%)
  local copies, waits for them, and re-layouts  5.18 us (16%)
    pallas_call x1, Pallas kernels, shards(): pl.pallas_call(body, out_shape=jax.ShapeDtypeStruct((rows_here // heads,...  27.1 us
    unnamed x11, local copies, waits for them, and re-layouts  5.18 us

profile of v1, /device:TPU:13, one launch (start us, length us, event | category | flops | bytes accessed | tf_op | source)
XLA Modules:
  0.0 32.3 jit_solution(1994383585696412600)
XLA Ops:
  0.0 0.0 copy-start
  0.0 1.2 %copy-done = bf16[128,4096]{1,0:T(8,128)(2,1)S(1)} copy-done((bf16[128,4096]{1,0:T(8,128)(2,1)S(1)}, bf16[128,4096]{1,0:T(8,128)(2,1)}, u32[]{:S(2)}) %copy-start) | copy-done | bytes 1048600
  1.2 0.0 copy-start.1
  1.2 0.8 %copy-done.1 = bf16[128,256]{1,0:T(8,128)(2,1)S(1)} copy-done((bf16[128,256]{1,0:T(8,128)(2,1)S(1)}, bf16[128,256]{1,0:T(8,128)(2,1)}, u32[]{:S(2)}) %copy-start.1) | copy-done | bytes 65560
  2.1 0.0 copy-start.2
  2.1 0.8 %copy-done.2 = bf16[128,256]{1,0:T(8,128)(2,1)S(1)} copy-done((bf16[128,256]{1,0:T(8,128)(2,1)S(1)}, bf16[128,256]{1,0:T(8,128)(2,1)}, u32[]{:S(2)}) %copy-start.2) | copy-done | bytes 65560
  2.9 0.0 copy-start.3
  2.9 0.7 %copy-done.3 = s32[10]{0:T(128)S(1)} copy-done((s32[10]{0:T(128)S(1)}, s32[10]{0:T(128)}, u32[]{:S(2)}) %copy-start.3) | copy-done | bytes 64
  3.6 0.0 copy-start.4
  3.6 0.7 %copy-done.4 = s32[8]{0:T(128)S(1)} copy-done((s32[8]{0:T(128)S(1)}, s32[8]{0:T(128)}, u32[]{:S(2)}) %copy-start.4) | copy-done | bytes 56
  4.2 27.1 %shard_map.55 = bf16[32,16384]{1,0:T(8,128)(2,1)S(1)} custom-call(s32[10]{0:T(128)S(1)} %copy-done.3, s32[8]{0:T(128)S(1)} %copy-done.4, bf16[128,4096]{1,0:T(8,128)(2,1)S(1)} %copy-done, bf16[128,256]{1,0:T(8,128)(2,1)S(1)} %copy-done.1, bf16[128,256]{1,0:T(8,128)(2,1)S(1)} %copy-done.2), custom_call_target="tpu_custom_call" | custom-call | tf_op jit(solution)/shard_map/pallas_call | solution.py:239
  31.3 1.0 %copy.7 = bf16[32,16384]{1,0:T(8,128)(2,1)} copy(bf16[32,16384]{1,0:T(8,128)(2,1)S(1)} %shard_map.55) | data formatting | bytes 2097152
Async XLA Ops:
  0.0 1.2 %copy-start = (bf16[128,4096]{1,0:T(8,128)(2,1)S(1)}, bf16[128,4096]{1,0:T(8,128)(2,1)}, u32[]{:S(2)}) copy-start(bf16[128,4096]{1,0:T(8,128)(2,1)} %q_hbm.1) | copy-start | bytes 3145732
  1.2 0.8 %copy-start.1 = (bf16[128,256]{1,0:T(8,128)(2,1)S(1)}, bf16[128,256]{1,0:T(8,128)(2,1)}, u32[]{:S(2)}) copy-start(bf16[128,256]{1,0:T(8,128)(2,1)} %k_ref.1) | copy-start | bytes 196612
  2.1 0.8 %copy-start.2 = (bf16[128,256]{1,0:T(8,128)(2,1)S(1)}, bf16[128,256]{1,0:T(8,128)(2,1)}, u32[]{:S(2)}) copy-start(bf16[128,256]{1,0:T(8,128)(2,1)} %v_ref.1) | copy-start | bytes 196612
  2.9 0.7 %copy-start.3 = (s32[10]{0:T(128)S(1)}, s32[10]{0:T(128)}, u32[]{:S(2)}) copy-start(s32[10]{0:T(128)} %lengths_ref.1) | copy-start | bytes 124
  3.6 0.7 %copy-start.4 = (s32[8]{0:T(128)S(1)}, s32[8]{0:T(128)}, u32[]{:S(2)}) copy-start(s32[8]{0:T(128)} %first_ref.1) | copy-start | bytes 100

commit v2 on v1

--- a/solution.py
+++ b/solution.py
@@ -22,7 +22,8 @@
 
 def kernel(
     pairs, heads, span, kv_local, per_group, chunk, tile,
-    lengths_ref, first_ref, q_hbm, k_ref, v_ref, out_ref,
+    lengths_hbm, first_hbm, q_hbm, k_hbm, v_hbm, out_ref,
+    lengths_ref, first_ref, k_ref, v_ref, in_sem,
     q_buf, own, upper, windows, bias, obuf,
     q_sem, up_send, up_recv, down_send, down_recv, out_send, out_recv, self_sem,
 ):
@@ -36,6 +37,14 @@
     width = chunk * DH
     keys_seen = (span + 1) * block
 
+    loads = [
+        pltpu.make_async_copy(source, target, in_sem.at[i])
+        for i, (source, target) in enumerate(
+            [(k_hbm, k_ref), (v_hbm, v_ref), (first_hbm, first_ref), (lengths_hbm, lengths_ref)]
+        )
+    ]
+    for load in loads:
+        load.start()
     load_q = pltpu.make_async_copy(q_hbm, q_buf, q_sem)
     load_q.start()
 
@@ -53,6 +62,8 @@
         pl.semaphore_signal(
             barrier, inc=1, device_id={"head": lax.rem(group + step, heads)}, device_id_type=MESH
         )
+    for load in loads:
+        load.wait()
     for h in range(kv_local):
         own[h, :, :DH] = k_ref[:, h * DH : (h + 1) * DH]
         own[h, :, DH:] = v_ref[:, h * DH : (h + 1) * DH]
@@ -233,17 +244,20 @@
     body = functools.partial(
         kernel, pairs, heads, span, kv_local, per_group, chunk, tile
     )
-    vmem = pl.BlockSpec(memory_space=pltpu.VMEM)
-    smem = pl.BlockSpec(memory_space=pltpu.SMEM)
-    hbm = pl.BlockSpec(memory_space=pl.ANY)
+    hbm = pl.BlockSpec(memory_space=pltpu.HBM)
     return pl.pallas_call(
         body,
         out_shape=jax.ShapeDtypeStruct(
             (rows_here // heads, queries.shape[1] * heads), jnp.bfloat16
         ),
-        in_specs=[smem, smem, hbm, vmem, vmem],
+        in_specs=[hbm] * 5,
         out_specs=hbm,
         scratch_shapes=[
+            pltpu.SMEM(lengths.shape, jnp.int32),
+            pltpu.SMEM(first_block.shape, jnp.int32),
+            pltpu.VMEM(keys.shape, jnp.bfloat16),
+            pltpu.VMEM(values.shape, jnp.bfloat16),
+            pltpu.SemaphoreType.DMA((4,)),
             pltpu.VMEM(queries.shape, jnp.bfloat16),
             pltpu.VMEM((kv_local, rows_here, 2 * DH), jnp.bfloat16),
             pltpu.VMEM((kv_local, span, rows_here, 2 * DH), jnp.bfloat16),
@@ -260,7 +274,7 @@
             pltpu.SemaphoreType.DMA((count,)),
         ],
         compiler_params=pltpu.CompilerParams(
-            collective_id=0, has_side_effects=True, vmem_limit_bytes=32 * 2**20
+            collective_id=0, has_side_effects=True, vmem_limit_bytes=62 * 2**20
         ),
     )(lengths, first_block, queries, keys, values)
 

time: 32.6 us -> 29.1 us (0.89)
  local copies, waits for them, and re-layouts: 5.18 us -> 2.26 us
  Pallas kernels: 27.1 us -> 26.6 us
    unnamed x11 -> x1, local copies, waits for them, and re-layouts: 5.18 us -> 2.26 us
    pallas_call x1, Pallas kernels: 27.1 us -> 26.6 us  [shards(): pl.pallas_call(body, out_shape=jax.ShapeDtypeStruct((rows_here // heads,...]
where the time goes in v2:
time: 29.1 us; the launch traced here: 28.9 us
  Pallas kernels  26.6 us (91%)
  local copies, waits for them, and re-layouts  2.26 us (8%)
    pallas_call x1, Pallas kernels, shards(): pl.pallas_call(body, out_shape=jax.ShapeDtypeStruct((rows_here // heads,...  26.6 us
    unnamed x1, local copies, waits for them, and re-layouts  2.26 us

profile of v2, /device:TPU:13, one launch (start us, length us, event | category | flops | bytes accessed | tf_op | source)
XLA Modules:
  0.0 28.9 jit_solution(11187461384981661036)
XLA Ops:
  0.0 26.6 %shard_map.55 = bf16[32,16384]{1,0:T(8,128)(2,1)} custom-call(s32[10]{0:T(128)} %lengths_hbm.1, s32[8]{0:T(128)} %first_hbm.1, bf16[128,4096]{1,0:T(8,128)(2,1)} %q_hbm.1, bf16[128,256]{1,0:T(8,128)(2,1)} %k_hbm.1, bf16[128,256]{1,0:T(8,128)(2,1)} %v_hbm.1), custom_call_target="tpu_custom_call" | custom-call | tf_op jit(solution)/shard_map/pallas_call | solution.py:248
  26.6 2.3 %copy.7 = bf16[32,16384]{1,0:T(8,128)(2,1)} copy(bf16[32,16384]{1,0:T(8,128)(2,1)} %shard_map.55) | data formatting | bytes 2097152
